TPU v7x, 256 devices: a whole 4x4x8 slice. The times are simulated.
256 devices in a mesh: seq: 64 (over y, z, core), kvh: 4 (over x).
Axes of the slice: x: 4, y: 4, z: 8, core: 2. Of those that a mesh axis runs over, the one named last changes fastest.
Arguments:
- queries: bfloat16 [128, 64, 128], P('seq', 'kvh')
- cache_keys: bfloat16 [131072, 8, 128], P('seq', 'kvh'), may hold values from -6 to 6
- cache_values: bfloat16 [131072, 8, 128], P('seq', 'kvh'), may hold values from -6 to 6
- new_keys: bfloat16 [128, 8, 128], P('seq', 'kvh'), may hold values from -6 to 6
- new_values: bfloat16 [128, 8, 128], P('seq', 'kvh'), may hold values from -6 to 6
- doc_start: int32 [128, 2], replicated, may hold values from 0 to 255, as said below
- doc_count: int32 [128, 2], replicated, may hold values from 1 to 64
Outputs:
- attended: bfloat16 [128, 64, 128], P('seq', 'kvh')
Inputs may be any that keep to these rules, and one draw needn't show every extreme that they name: doc_start[r, i] + doc_count[r, i] <= 256.
All inputs are finite; a program needn't handle non-finite values.
Results may differ from a plain program's by a relative error of at most 0.0048.
Values may be sent and summed in bfloat16 or wider, within the bound.
A program may use at most 256 MiB of HBM per device.

v0:
```python
import functools

import jax
import jax.numpy as jnp
from jax import lax
from jax.experimental import pallas as pl
from jax.experimental.pallas import tpu as pltpu
from jax.sharding import PartitionSpec as P

MESH = pl.DeviceIdType.MESH
HD = 128
BLOCK = 512
NBLOCKS = 4
TOK = BLOCK * NBLOCKS
NEG = -1e30
SCALE = HD ** (-0.5)
F32 = jnp.float32
BF16 = jnp.bfloat16


def lanes_of(rows):
    return lax.broadcasted_iota(jnp.int32, (rows, 128), 1)


def encode(stat, count):
    stat = jnp.where(lanes_of(16) < count, stat, 0.0)
    high = stat.astype(BF16).astype(F32)
    rest = stat - high
    middle = rest.astype(BF16).astype(F32)
    low = rest - middle
    return high + pltpu.roll(middle, 32, 1) + pltpu.roll(low, 64, 1)


def decode(tile):
    tile = tile.astype(F32)
    return tile + pltpu.roll(tile, 96, 1) + pltpu.roll(tile, 64, 1)


def weights_of(stats):
    top = functools.reduce(jnp.maximum, stats)
    raw = [jnp.exp(s - top) for s in stats]
    total = functools.reduce(jnp.add, raw)
    inverse = 1.0 / total
    return [w * inverse for w in raw], top + jnp.log(total)


def two_columns(weight, g, column):
    part = weight[g * 8 : (g + 1) * 8]
    return jnp.concatenate(
        [jnp.broadcast_to(part[:, column + r : column + r + 1], (8, 128)) for r in range(2)], axis=0
    )


def by_distance(n, first=1):
    return sorted(range(first, n), key=lambda k: -min(k, n - k))


def kernel(
    ny, nz,
    q_hbm, k_hbm, v_hbm, nk_hbm, nv_hbm, start_hbm, count_hbm, out_ref,
    q_ref, nk_ref, nv_ref, start_ref, count_ref,
    q_mine, qbuf, bias, kraw, vraw, temp, kaug, vaug, scores,
    y_out, y_in, z_out, z_in,
    load_sem, kv_send, kv_recv, qz_send, qz_recv, qy_send, qy_recv,
    y_send, y_recv, z_send, z_recv,
):
    half = nz // 2
    pair = half // 2
    seq = lax.axis_index("seq")
    x = lax.axis_index("kvh")
    core = lax.rem(seq, 2)
    z = lax.rem(lax.div(seq, 2), nz)
    y = lax.div(seq, 2 * nz)
    other = 1 - core
    hub = 1 - lax.div(z, half)
    is_hub = hub == core
    place = lax.rem(z, half)
    base = (1 - core) * half

    def device(yy, zz, cc):
        return ((yy * nz + zz) * 2 + cc, x)

    def along(i):
        return lax.rem(y + i, ny)

    def around(i):
        return lax.rem(z + i, nz)

    def remote(src, dst, send, recv, peer):
        return pltpu.make_async_remote_copy(
            src_ref=src, dst_ref=dst, send_sem=send, recv_sem=recv, device_id=peer, device_id_type=MESH
        )

    loads = [
        pltpu.make_async_copy(src, dst, load_sem.at[i])
        for i, (src, dst) in enumerate(
            [
                (q_hbm, q_ref), (start_hbm, start_ref), (count_hbm, count_ref),
                (k_hbm, kraw.at[0]), (v_hbm, vraw.at[0]), (nk_hbm, nk_ref), (nv_hbm, nv_ref),
            ]
        )
    ]
    for load in loads:
        load.start()

    barrier = pltpu.get_barrier_semaphore()

    def greet(peer):
        pl.semaphore_signal(barrier, inc=1, device_id=peer, device_id_type=MESH)

    for k in by_distance(nz):
        greet(device(y, around(k), hub))
    for i in range(half):
        greet(device(y, base + lax.rem(place + half - 1 - i, half), 1 - hub))
    for k in by_distance(ny):
        greet(device(along(k), z, core))

    @pl.when(hub != core)
    def _():
        greet(device(y, z, hub))

    loads[0].wait()
    q_own = q_ref[...].astype(F32)
    for g in range(2):
        q_mine[g] = jnp.concatenate([q_own[r, g * 8 : (g + 1) * 8] for r in range(2)], axis=0).astype(BF16)

    @pl.when(is_hub)
    def _():
        qbuf[y, place, core] = q_mine[...]

    pl.semaphore_wait(barrier, nz - 1 + half + ny - 1 + jnp.abs(hub - core))

    def qz_copy(k):
        return remote(
            q_mine, qbuf.at[y, place, core], qz_send.at[k], qz_recv.at[place, core], device(y, around(k), hub)
        )

    for k in by_distance(nz):
        qz_copy(k).start()

    @pl.when(hub != core)
    def _():
        qz_copy(0).start()

    swaps = [
        remote(src, dst, kv_send.at[i], kv_recv.at[i], device(y, z, other))
        for i, (src, dst) in enumerate([(k_hbm, kraw.at[1]), (v_hbm, vraw.at[1])])
    ]
    for swap in swaps:
        swap.start()

    lane = lanes_of(8)
    block = jnp.where(lane < NBLOCKS, seq * NBLOCKS + lane, (seq + 1 - 2 * core) * NBLOCKS + lane - NBLOCKS)

    def row_bias(row):
        seen = None
        for i in range(2):
            first = start_ref[i, row]
            inside = (block >= first) & (block < first + count_ref[i, row])
            seen = inside if seen is None else seen | inside
        return jnp.where(seen | (lane >= 2 * NBLOCKS), 0.0, NEG)

    def fill_bias(i, carry):
        yy, zi, cc = lax.div(i, nz), lax.rem(lax.div(i, 2), half), lax.rem(i, 2)
        row = 4 * (yy * nz + base + zi) + 2 * cc
        bias[yy, zi, cc] = jnp.concatenate([row_bias(row), row_bias(row + 1)], axis=0).astype(BF16)
        return carry

    loads[1].wait()
    loads[2].wait()
    lax.fori_loop(0, ny * nz, fill_bias, 0)

    piece = 256

    def split(which):
        def body(i, carry):
            at = pl.multiple_of(which * TOK + i * piece, piece)
            flat = pl.multiple_of(i * 2 * piece, 2 * piece)
            indicator = (lanes_of(piece) == lax.div(at, BLOCK)).astype(F32).astype(BF16)
            temp[0] = kraw[which, pl.ds(flat, 2 * piece), :].astype(F32)
            temp[1] = vraw[which, pl.ds(flat, 2 * piece), :].astype(F32)
            for g in range(2):
                kaug[g, pl.ds(at, piece), 0:128] = temp[0, pl.ds(g, piece, stride=2), :].astype(BF16)
                kaug[g, pl.ds(at, piece), 128:256] = indicator
                vaug[g, pl.ds(at, piece), 0:128] = temp[1, pl.ds(g, piece, stride=2), :].astype(BF16)
                vaug[g, pl.ds(at, piece), 128:256] = jnp.ones((piece, 128), BF16)
            return carry

        lax.fori_loop(0, TOK // piece, body, 0)

    loads[3].wait()
    loads[4].wait()
    split(0)

    def qy_copy(w, k):
        mine = qbuf.at[y, pl.ds(w * pair, pair)]
        return remote(mine, mine, qy_send.at[w, k - 1], qy_recv.at[w, k - 1], device(along(k), z, core))

    def qy_arrival(w, k):
        there = qbuf.at[along(ny - k), pl.ds(w * pair, pair)]
        return remote(there, there, qy_send.at[w, k - 1], qy_recv.at[w, k - 1], device(along(k), z, core))

    for w in range(2):
        for zi in range(w * pair, (w + 1) * pair):
            for cc in range(2):

                @pl.when((base + zi != z) | (core != cc))
                def _():
                    there = qbuf.at[y, zi, cc]
                    remote(
                        there, there, qz_send.at[0], qz_recv.at[zi, cc], device(along(1), z, core)
                    ).wait_recv()

        for k in by_distance(ny):
            qy_copy(w, k).start()

    for swap in swaps:
        swap.wait_recv()
    split(1)

    rows = 32 * pair
    count = 4 * pair

    def attend(w):
        tops = []
        for g in range(2):
            lhs = jnp.concatenate(
                [
                    qbuf[:, pl.ds(w * pair, pair), :, g].reshape(ny * rows, 128),
                    bias[:, pl.ds(w * pair, pair)].reshape(ny * rows, 128),
                ],
                axis=1,
            )
            top = None
            for b in range(2 * NBLOCKS):
                s = lax.dot_general(
                    lhs, kaug[g, b * BLOCK : (b + 1) * BLOCK, :], (((1,), (1,)), ((), ())),
                    preferred_element_type=F32,
                )
                scores[g, :, b * BLOCK : (b + 1) * BLOCK] = s
                for i in range(BLOCK // 128):
                    part = s[:, i * 128 : (i + 1) * 128]
                    top = part if top is None else jnp.maximum(top, part)
            tops.append(jnp.max(top, axis=1, keepdims=True))
        stats = [[None] * 2 for _ in range(ny)]
        for g in range(2):
            total = None
            for b in range(2 * NBLOCKS):
                s = scores[g, :, b * BLOCK : (b + 1) * BLOCK]
                p = jnp.exp((s - tops[g]) * SCALE).astype(BF16)
                term = jnp.dot(p, vaug[g, b * BLOCK : (b + 1) * BLOCK, :], preferred_element_type=F32)
                total = term if total is None else total + term
            norm = total[:, 128:256]
            out = total[:, 0:128] * (1.0 / norm)
            stat = tops[g] * SCALE + jnp.log(norm)
            for yy in range(ny):
                packed = jnp.zeros((8, 128), F32)
                for k in range(count):
                    at = yy * rows + k * 8
                    packed = jnp.where(lane == k, stat[at : at + 8], packed)
                stats[yy][g] = packed
                for i in range(count // 2):
                    at = yy * rows + i * 16
                    y_out[w, yy, i * 2 + g] = out[at : at + 16].astype(BF16)
        for yy in range(ny):
            y_out[w, yy, count] = encode(jnp.concatenate(stats[yy], axis=0), count).astype(BF16)

    def y_copy(w, k):
        return remote(
            y_out.at[w, along(k)], y_in.at[w, k - 1], y_send.at[w, k - 1], y_recv.at[w, k - 1],
            device(along(k), z, core),
        )

    def forward(w, carry):
        for k in range(1, ny):
            qy_arrival(w, k).wait_recv()
        attend(w)
        for k in by_distance(ny):
            y_copy(w, k).start()
        return carry

    lax.fori_loop(0, 2, forward, 0)

    def z_copy(zi, cc):
        return remote(
            z_out.at[zi, cc], z_in.at[z], z_send.at[zi, cc], z_recv.at[z], device(y, base + zi, cc)
        )

    def back(w, carry):
        for k in range(1, ny):
            y_copy(w, k).wait_recv()
        parts = [y_out.at[w, y]] + [y_in.at[w, k] for k in range(ny - 1)]
        weights, stat = weights_of([decode(part[count]) for part in parts])
        stat = encode(stat, count)
        for i in range(count // 2):
            zi, cc = w * pair + i // 2, i % 2
            for g in range(2):
                tile = None
                for part, weight in zip(parts, weights):
                    term = part[i * 2 + g].astype(F32) * two_columns(weight, g, 2 * i)
                    tile = term if tile is None else tile + term
                z_out[zi, cc, g] = tile.astype(BF16)
            z_out[zi, cc, 2] = (stat if i == 0 else pltpu.roll(stat, 128 - 2 * i, 1)).astype(BF16)
        for i in range(count // 2):
            zi, cc = w * pair + i // 2, i % 2

            @pl.when((base + zi != z) | (core != cc))
            def _():
                z_copy(zi, cc).start()

        return carry

    lax.fori_loop(0, 2, back, 0)

    loads[5].wait()
    loads[6].wait()

    @pl.when(is_hub)
    def _():
        z_in[z] = z_out[place, core]

    own = [None, None]
    for g in range(2):
        packed = jnp.zeros((8, 128), F32)
        for r in range(2):
            key = nk_ref[r].astype(F32)[g : g + 1]
            dots = jnp.sum(q_own[r, g * 8 : (g + 1) * 8] * key, axis=1, keepdims=True) * SCALE
            packed = jnp.where(lane == r, dots, packed)
        own[g] = packed
    own = jnp.concatenate(own, axis=0)

    for k in range(nz):
        zz = around(k)

        @pl.when((hub != core) | (zz != z))
        def _():
            there = z_in.at[zz]
            remote(there, there, z_send.at[0, 0], z_recv.at[zz], device(along(1), z, core)).wait_recv()

    parts = [z_in.at[k] for k in range(nz)]
    weights, _ = weights_of([decode(part[2]) for part in parts] + [own])
    tiles = []
    for g in range(2):
        tile = None
        for part, weight in zip(parts, weights):
            term = part[g].astype(F32) * two_columns(weight, g, 0)
            tile = term if tile is None else tile + term
        value = jnp.concatenate(
            [jnp.broadcast_to(nv_ref[r].astype(F32)[g : g + 1], (8, 128)) for r in range(2)], axis=0
        )
        tiles.append(tile + value * two_columns(weights[-1], g, 0))
    for r in range(2):
        out_ref[r] = jnp.concatenate([tiles[g][r * 8 : (r + 1) * 8] for g in range(2)], axis=0).astype(BF16)

    for swap in swaps:
        swap.wait_send()
    for k in range(1, nz):
        qz_copy(k).wait_send()

    @pl.when(hub != core)
    def _():
        qz_copy(0).wait_send()

    for zi in range(half):
        for cc in range(2):

            @pl.when((base + zi != z) | (core != cc))
            def _():
                z_copy(zi, cc).wait_send()

    for k in range(1, ny):
        for w in range(2):
            qy_copy(w, k).wait_send()
            y_copy(w, k).wait_send()


def per_device(ny, nz, queries, cache_keys, cache_values, new_keys, new_values, doc_start, doc_count):
    hbm = pl.BlockSpec(memory_space=pltpu.HBM)
    dma = pltpu.SemaphoreType.DMA
    half = nz // 2
    pair = half // 2
    tiles = 4 * pair + 1
    return pl.pallas_call(
        functools.partial(kernel, ny, nz),
        out_shape=pltpu.VMEM(queries.shape, BF16),
        in_specs=[hbm] * 7,
        out_specs=pl.BlockSpec(memory_space=pltpu.VMEM),
        scratch_shapes=[
            pltpu.VMEM(queries.shape, BF16),
            pltpu.VMEM(new_keys.shape, BF16),
            pltpu.VMEM(new_values.shape, BF16),
            pltpu.SMEM(doc_start.shape[::-1], jnp.int32),
            pltpu.SMEM(doc_count.shape[::-1], jnp.int32),
            pltpu.VMEM((2, 16, 128), BF16),
            pltpu.VMEM((ny, half, 2, 2, 16, 128), BF16),
            pltpu.VMEM((ny, half, 2, 16, 128), BF16),
            pltpu.VMEM((2, 2 * TOK, 128), BF16),
            pltpu.VMEM((2, 2 * TOK, 128), BF16),
            pltpu.VMEM((2, 512, 128), F32),
            pltpu.VMEM((2, 2 * TOK, 256), BF16),
            pltpu.VMEM((2, 2 * TOK, 256), BF16),
            pltpu.VMEM((2, 32 * pair * ny, 2 * TOK), F32),
            pltpu.VMEM((2, ny, tiles, 16, 128), BF16),
            pltpu.VMEM((2, ny - 1, tiles, 16, 128), BF16),
            pltpu.VMEM((half, 2, 3, 16, 128), BF16),
            pltpu.VMEM((nz, 3, 16, 128), BF16),
            dma((7,)),
            dma((2,)), dma((2,)),
            dma((nz,)), dma((half, 2)),
            dma((2, ny - 1)), dma((2, ny - 1)),
            dma((2, ny - 1)), dma((2, ny - 1)),
            dma((half, 2)), dma((nz,)),
        ],
        compiler_params=pltpu.CompilerParams(
            collective_id=0, has_side_effects=True, vmem_limit_bytes=60 * 1024 * 1024
        ),
        name="attention",
    )(
        queries,
        cache_keys.reshape(2 * TOK, 128),
        cache_values.reshape(2 * TOK, 128),
        new_keys,
        new_values,
        doc_start.T,
        doc_count.T,
    )


def solution(mesh):
    ny, nz = 4, mesh.shape["seq"] // 8
    placed = (P("seq", "kvh", None),) * 5 + (P(), P())
    return jax.shard_map(
        functools.partial(per_device, ny, nz),
        mesh=mesh,
        in_specs=placed,
        out_specs=P("seq", "kvh", None),
        check_vma=False,
    )
```

profile of v0, /device:TPU:65, one launch (start us, length us, event | category | flops | bytes accessed | tf_op | source)
XLA Modules:
  0.0 29.2 jit_solution(3318332005803050676)
XLA Ops:
  0.0 28.6 %attention.1 = bf16[2,16,128]{2,1,0:T(8,128)(2,1)S(1)} custom-call(bf16[2,16,128]{2,1,0:T(8,128)(2,1)} %q_hbm.1, bf16[4096,128]{1,0:T(8,128)(2,1)} %bitcast.4, bf16[4096,128]{1,0:T(8,128)(2,1)} %bitcast.5, bf16[2,2,128]{2,1,0:T(2,128)(2,1)} %nk_hbm.1, bf16[2,2,128]{2,1,0:T(2,128)(2,1)} %nv_hbm.1, s32[2,128]{1,0:T(2,128)} %bitcast.6, s32[2,128]{1,0:T(2,128)} %bitcast.7), custom_call_target="tpu_custom_call" | custom-call | tf_op jit(solution)/shard_map/attention/pallas_call | solution.py:383
  28.6 0.6 %copy.9 = bf16[2,16,128]{2,1,0:T(8,128)(2,1)} copy(bf16[2,16,128]{2,1,0:T(8,128)(2,1)S(1)} %attention.1) | data formatting | bytes 16384
where the time goes:
time: 29.3 us; the launch traced here: 29.2 us
  Pallas kernels  28.6 us (98%)
  local copies, waits for them, and re-layouts  0.6 us (2%)
    pallas_call x1, Pallas kernels, per_device(): pl.pallas_call(functools.partial(kernel, ny, nz), out_shape=pltpu.VMEM(qu...  28.6 us
    unnamed x1, local copies, waits for them, and re-layouts  0.6 us

commit v1 on v0

--- a/solution.py
+++ b/solution.py
@@ -100,8 +100,7 @@
             ]
         )
     ]
-    for load in loads:
-        load.start()
+    loads[0].start()
 
     barrier = pltpu.get_barrier_semaphore()
 
@@ -109,15 +108,18 @@
         pl.semaphore_signal(barrier, inc=1, device_id=peer, device_id_type=MESH)
 
     for k in by_distance(nz):
-        greet(device(y, around(k), hub))
-    for i in range(half):
-        greet(device(y, base + lax.rem(place + half - 1 - i, half), 1 - hub))
+        zz = around(k)
+        greet(device(y, zz, hub))
+
+        @pl.when(lax.div(zz, half) == 1 - core)
+        def _():
+            greet(device(y, zz, 1 - hub))
+
     for k in by_distance(ny):
         greet(device(along(k), z, core))
-
-    @pl.when(hub != core)
-    def _():
-        greet(device(y, z, hub))
+    greet(device(y, z, other))
+    for load in loads[1:]:
+        load.start()
 
     loads[0].wait()
     q_own = q_ref[...].astype(F32)
@@ -265,18 +267,21 @@
         for yy in range(ny):
             y_out[w, yy, count] = encode(jnp.concatenate(stats[yy], axis=0), count).astype(BF16)
 
-    def y_copy(w, k):
+    def y_copy(w, yy):
         return remote(
-            y_out.at[w, along(k)], y_in.at[w, k - 1], y_send.at[w, k - 1], y_recv.at[w, k - 1],
-            device(along(k), z, core),
+            y_out.at[w, yy], y_in.at[w, y], y_send.at[w, yy], y_recv.at[w, y], device(yy, z, core)
         )
 
     def forward(w, carry):
         for k in range(1, ny):
             qy_arrival(w, k).wait_recv()
         attend(w)
-        for k in by_distance(ny):
-            y_copy(w, k).start()
+        for yy in range(ny):
+
+            @pl.when(yy != y)
+            def _():
+                y_copy(w, yy).start()
+
         return carry
 
     lax.fori_loop(0, 2, forward, 0)
@@ -288,8 +293,9 @@
 
     def back(w, carry):
         for k in range(1, ny):
-            y_copy(w, k).wait_recv()
-        parts = [y_out.at[w, y]] + [y_in.at[w, k] for k in range(ny - 1)]
+            there = y_in.at[w, along(k)]
+            remote(there, there, y_send.at[w, 0], y_recv.at[w, along(k)], device(along(k), z, core)).wait_recv()
+        parts = [y_out.at[w, y]] + [y_in.at[w, along(k)] for k in range(1, ny)]
         weights, stat = weights_of([decode(part[count]) for part in parts])
         stat = encode(stat, count)
         for i in range(count // 2):
@@ -371,7 +377,7 @@
     for k in range(1, ny):
         for w in range(2):
             qy_copy(w, k).wait_send()
-            y_copy(w, k).wait_send()
+            y_copy(w, along(k)).wait_send()
 
 
 def per_device(ny, nz, queries, cache_keys, cache_values, new_keys, new_values, doc_start, doc_count):
@@ -401,14 +407,14 @@
             pltpu.VMEM((2, 2 * TOK, 256), BF16),
             pltpu.VMEM((2, 32 * pair * ny, 2 * TOK), F32),
             pltpu.VMEM((2, ny, tiles, 16, 128), BF16),
-            pltpu.VMEM((2, ny - 1, tiles, 16, 128), BF16),
+            pltpu.VMEM((2, ny, tiles, 16, 128), BF16),
             pltpu.VMEM((half, 2, 3, 16, 128), BF16),
             pltpu.VMEM((nz, 3, 16, 128), BF16),
             dma((7,)),
             dma((2,)), dma((2,)),
             dma((nz,)), dma((half, 2)),
             dma((2, ny - 1)), dma((2, ny - 1)),
-            dma((2, ny - 1)), dma((2, ny - 1)),
+            dma((2, ny)), dma((2, ny)),
             dma((half, 2)), dma((nz,)),
         ],
         compiler_params=pltpu.CompilerParams(

time: 29.3 us -> 29.1 us (level)
  the two profiles are of different devices: /device:TPU:65 before, /device:TPU:1 now
where the time goes in v1:
time: 29.1 us; the launch traced here: 28.7 us
  Pallas kernels  28.1 us (97%)
  local copies, waits for them, and re-layouts  0.6 us (2%)
    pallas_call x1, Pallas kernels, per_device(): pl.pallas_call(functools.partial(kernel, ny, nz), out_shape=pltpu.VMEM(qu...  28.1 us
    unnamed x1, local copies, waits for them, and re-layouts  0.6 us

profile of v1, /device:TPU:1, one launch (start us, length us, event | category | flops | bytes accessed | tf_op | source)
XLA Modules:
  0.0 28.7 jit_solution(3014848255606940907)
XLA Ops:
  0.0 28.1 %attention.1 = bf16[2,16,128]{2,1,0:T(8,128)(2,1)S(1)} custom-call(bf16[2,16,128]{2,1,0:T(8,128)(2,1)} %q_hbm.1, bf16[4096,128]{1,0:T(8,128)(2,1)} %bitcast.4, bf16[4096,128]{1,0:T(8,128)(2,1)} %bitcast.5, bf16[2,2,128]{2,1,0:T(2,128)(2,1)} %nk_hbm.1, bf16[2,2,128]{2,1,0:T(2,128)(2,1)} %nv_hbm.1, s32[2,128]{1,0:T(2,128)} %bitcast.6, s32[2,128]{1,0:T(2,128)} %bitcast.7), custom_call_target="tpu_custom_call" | custom-call | tf_op jit(solution)/shard_map/attention/pallas_call | solution.py:389
  28.1 0.6 %copy.9 = bf16[2,16,128]{2,1,0:T(8,128)(2,1)} copy(bf16[2,16,128]{2,1,0:T(8,128)(2,1)S(1)} %attention.1) | data formatting | bytes 16384
